TPU v7x, 32 devices: a whole 2x2x4 slice. The times are simulated.
32 devices in a mesh: head: 2 (over x), seq: 16 (over z, y, core).
Axes of the slice: x: 2, y: 2, z: 4, core: 2. Of those that a mesh axis runs over, the one named last changes fastest.
Arguments:
- queries: bfloat16 [2048, 3072], P(('head', 'seq')), may hold values from -6 to 6
- key_rows: bfloat16 [12288, 3072], P('seq', 'head'), may hold values from -6 to 6
- values: bfloat16 [12288, 3072], P('seq', 'head'), may hold values from -6 to 6
- w_out: bfloat16 [3072, 6144], P('head'), may hold values from -1.1953125 to 1.1953125
- picked: int32 [32, 24], replicated, may hold values from 0 to 191, as said below
- counts: int32 [32], replicated, may hold values from 8 to 24
- tile_home: int32 [192], replicated, may hold values from 0 to 191, as said below
Outputs:
- layer_out: bfloat16 [2048, 6144], P(('head', 'seq'))
Inputs may be any that keep to these rules, and one draw needn't show every extreme that they name: `picked`: query tiles j with the same j modulo the number of devices along seq form a group. The used entries of one group are distinct key tiles; key tile t is stored on owner tile_home[t] // 12, and at most 3 used entries of one group are stored on one owner, exactly 3 for some owner in every group. `tile_home`: A permutation of the key tiles.
All inputs are finite; a program needn't handle non-finite values.
Results may differ from a plain program's by a relative error of at most 0.009.
Values may be sent and summed in bfloat16 or wider, within the bound.
A program may use at most 128 MiB of HBM per device.

v0:
```python
import jax
import jax.numpy as jnp
from jax import lax
from jax.sharding import PartitionSpec as P

HD = 128
MAXSEL = 24


def body(queries, key_rows, values, w_out, picked, counts, tile_home):
    head_count = lax.axis_size("head")
    seq_count = lax.axis_size("seq")
    seq_index = lax.axis_index("seq")
    tile_rows = queries.shape[0]
    width_local = w_out.shape[0]
    heads_local = width_local // HD
    tiles_dev = key_rows.shape[0] // tile_rows
    capacity = max(2, head_count * MAXSEL // seq_count)
    request_count = head_count * MAXSEL
    local_queries = lax.all_to_all(queries, "head", split_axis=1, concat_axis=0, tiled=True)
    group_pick = (
        picked.reshape(head_count, seq_count, MAXSEL)
        .transpose(1, 0, 2)
        .reshape(seq_count, request_count)
    )
    group_count = counts.reshape(head_count, seq_count).transpose(1, 0)
    position = lax.broadcasted_iota(jnp.int32, (head_count, MAXSEL), 1).reshape(request_count)
    is_live = position[None, :] < jnp.repeat(group_count, MAXSEL, axis=1)
    stored = tile_home[group_pick]
    owner_of = stored // tiles_dev
    inside_offset = stored % tiles_dev
    owner_ids = lax.broadcasted_iota(jnp.int32, (1, 1, seq_count), 2)
    hit_table = ((owner_of[:, :, None] == owner_ids) & is_live[:, :, None]).astype(jnp.int32)
    before = jnp.cumsum(hit_table, axis=1) - hit_table
    slot_rank = jnp.sum(before * hit_table, axis=2)
    for_me = (owner_of == seq_index) & is_live
    slot_ids = lax.broadcasted_iota(jnp.int32, (1, 1, capacity), 2)
    slot_hits = (for_me[:, :, None] & (slot_rank[:, :, None] == slot_ids)).astype(jnp.int32)
    send_within = jnp.sum(slot_hits * inside_offset[:, :, None], axis=1)
    key_blocks = key_rows.reshape(tiles_dev, tile_rows, width_local)
    value_blocks = values.reshape(tiles_dev, tile_rows, width_local)
    send_keys = key_blocks[send_within]
    send_values = value_blocks[send_within]
    my_owner = lax.dynamic_index_in_dim(owner_of, seq_index, 0, keepdims=False)
    my_rank = lax.dynamic_index_in_dim(slot_rank, seq_index, 0, keepdims=False)
    my_live = lax.dynamic_index_in_dim(is_live, seq_index, 0, keepdims=False)
    flat_slot = my_owner * capacity + jnp.minimum(my_rank, capacity - 1)

    def arrange(incoming_rows):
        picked_rows = incoming_rows.reshape(seq_count * capacity, tile_rows, width_local)[flat_slot]
        return picked_rows.reshape(head_count, MAXSEL * tile_rows, heads_local, HD)

    query_heads = local_queries.reshape(head_count, tile_rows, heads_local, HD)
    key_live = jnp.repeat(my_live.reshape(head_count, MAXSEL), tile_rows, axis=1)[:, None, None, :]
    recv_keys, recv_values = (
        lax.all_to_all(send_keys, "seq", split_axis=0, concat_axis=0, tiled=True),
        lax.all_to_all(send_values, "seq", split_axis=0, concat_axis=0, tiled=True),
    )
    logit_scores = jnp.einsum(
        "rqhd,rkhd->rhqk", query_heads, arrange(recv_keys), preferred_element_type=jnp.float32
    ) * HD ** (-0.5)
    logit_scores = jnp.where(key_live, logit_scores, -1e30)
    row_top = jnp.max(logit_scores, axis=-1, keepdims=True)
    exponent = jnp.where(key_live, jnp.exp(logit_scores - row_top), 0.0)
    weights = exponent.astype(jnp.bfloat16)
    row_sum_total = jnp.sum(exponent, axis=-1)
    fetched_values = arrange(recv_values)
    mixed = jnp.einsum(
        "rhqk,rkhd->rqhd", weights, fetched_values, preferred_element_type=jnp.float32
    )
    mixed = mixed / jnp.transpose(row_sum_total, (0, 2, 1))[:, :, :, None]
    attended = mixed.astype(jnp.bfloat16).reshape(head_count * tile_rows, width_local)
    return lax.psum_scatter(
        jnp.dot(attended, w_out, preferred_element_type=jnp.float32).astype(jnp.bfloat16),
        "head",
        scatter_dimension=0,
        tiled=True,
    )


def solution(mesh):
    placed = (
        P(("head", "seq"), None),
        P("seq", "head"),
        P("seq", "head"),
        P("head", None),
        P(),
        P(),
        P(),
    )
    return jax.shard_map(
        body, mesh=mesh, in_specs=placed, out_specs=P(("head", "seq"), None), check_vma=False
    )
```

profile of v0, /device:TPU:26, one launch (start us, length us, event | category | flops | bytes accessed | tf_op | source)
XLA Modules:
  0.0 577.1 jit_solution(18341137012072334961)
XLA Ops:
  6.5 0.0 copy-start
  6.5 0.9 copy.52
  7.5 0.1 reshape.183
  7.6 0.1 reshape.196
  7.7 4.8 gather_fusion
  12.5 0.1 reshape.239
  12.6 0.1 copy.54
  12.7 0.1 reshape.241
  12.7 0.1 copy.56
  12.8 0.1 reshape.243
  12.9 0.1 copy.55
  13.0 0.1 lt.70
  13.1 0.7 reshape.184
  13.8 0.1 compare_and_fusion
  13.9 1.5 fusion.43
  15.4 0.1 copy.59
  15.5 0.1 copy.58
  15.6 0.1 copy.63
  15.7 0.2 select_reduce_fusion
  15.8 0.1 copy.64
  15.9 0.1 reshape.204
  16.0 0.0 copy-done
  16.0 6.4 %gather_fusion.3 = bf16[48,64,1536]{2,1,0:T(8,128)(2,1)} fusion(bf16[12,64,1536]{2,1,0:T(8,128)(2,1)S(1)} %bitcast.63, s32[1024]{0:T(1024)S(1)} %pad_clamp_fusion.1), kind=kCustom, calls=%fused_computation.3 | custom fusion | bytes 18874560 | tf_op jit(solution)/shard_map/gather | solution.py:42
  22.4 0.0 copy-start.2
  22.4 6.2 %all-to-all-start.1 = ((bf16[16,3,64,1536]{3,2,1,0:T(8,128)(2,1)}), bf16[16,3,64,1536]{3,2,1,0:T(8,128)(2,1)}, u32[]{:S(2)}, u32[]{:S(2)}) async-start(bf16[16,3,64,1536]{3,2,1,0:T(8,128)(2,1)} %bitcast.65), calls=%async_computation.1 | async-start | bytes 18874368 | tf_op jit(solution)/shard_map/all_to_all | solution.py:56
  28.6 0.0 copy-done.2
  28.6 6.4 %gather_fusion.1 = bf16[48,64,1536]{2,1,0:T(8,128)(2,1)} fusion(bf16[12,64,1536]{2,1,0:T(8,128)(2,1)S(1)} %bitcast.66, s32[1024]{0:T(1024)S(1)} %pad_clamp_fusion.1), kind=kCustom, calls=%fused_computation.1 | custom fusion | bytes 18874560 | tf_op jit(solution)/shard_map/gather | solution.py:43
  35.0 184.7 %all-to-all-done.1 = bf16[16,3,64,1536]{3,2,1,0:T(8,128)(2,1)} async-done(((bf16[16,3,64,1536]{3,2,1,0:T(8,128)(2,1)}), bf16[16,3,64,1536]{3,2,1,0:T(8,128)(2,1)}, u32[]{:S(2)}, u32[]{:S(2)}) %all-to-all-start.1) | async-done | bytes 9437216 | tf_op jit(solution)/shard_map/all_to_all | solution.py:56
  219.7 0.0 copy-start.3
  219.7 18.8 %all-to-all-start = ((bf16[16,3,64,1536]{3,2,1,0:T(8,128)(2,1)}), bf16[16,3,64,1536]{3,2,1,0:T(8,128)(2,1)}, u32[]{:S(2)}, u32[]{:S(2)}) async-start(bf16[16,3,64,1536]{3,2,1,0:T(8,128)(2,1)} %bitcast.64), calls=%async_computation | async-start | bytes 18874368 | tf_op jit(solution)/shard_map/all_to_all | solution.py:57
  238.5 0.0 copy-done.3
  238.5 0.8 copy.92
  239.3 0.2 add_reduce_fusion
  239.4 190.1 %all-to-all-done = bf16[16,3,64,1536]{3,2,1,0:T(8,128)(2,1)} async-done(((bf16[16,3,64,1536]{3,2,1,0:T(8,128)(2,1)}), bf16[16,3,64,1536]{3,2,1,0:T(8,128)(2,1)}, u32[]{:S(2)}, u32[]{:S(2)}) %all-to-all-start) | async-done | bytes 9437216 | tf_op jit(solution)/shard_map/all_to_all | solution.py:57
  429.5 4.0 all-to-all-start.2
  433.5 0.0 reduce-scatter.2.cloned.1.call-start
  433.5 0.2 dynamic-slice_reduce_fusion
  433.7 0.1 reshape.188
  433.8 0.1 broadcast_in_dim.41
  433.9 0.1 broadcast_in_dim.42
  434.0 10.1 %gather_fusion.4 = bf16[48,64,1536]{2,1,0:T(8,128)(2,1)} fusion(bf16[48,64,1536]{2,1,0:T(8,128)(2,1)} %bitcast.11, s32[1024]{0:T(1024)S(1)} %pad_clamp_fusion), kind=kCustom, calls=%fused_computation.4 | custom fusion | bytes 18874560 | tf_op jit(solution)/shard_map/gather | solution.py:50
  444.1 17.8 %reshape.191 = bf16[2,1536,12,128]{3,2,1,0:T(8,128)(2,1)} reshape(bf16[48,64,1536]{2,1,0:T(8,128)(2,1)} %gather_fusion.4) | data formatting | bytes 18874368 | tf_op jit(solution)/shard_map/reshape | solution.py:51
  461.9 10.0 %gather_fusion.2 = bf16[48,64,1536]{2,1,0:T(8,128)(2,1)} fusion(bf16[48,64,1536]{2,1,0:T(8,128)(2,1)} %bitcast.7, s32[1024]{0:T(1024)S(1)} %pad_clamp_fusion), kind=kCustom, calls=%fused_computation.2 | custom fusion | bytes 18874560 | tf_op jit(solution)/shard_map/gather | solution.py:50
  471.9 17.8 %reshape.187 = bf16[2,1536,12,128]{3,2,1,0:T(8,128)(2,1)} reshape(bf16[48,64,1536]{2,1,0:T(8,128)(2,1)} %gather_fusion.2) | data formatting | bytes 18874368 | tf_op jit(solution)/shard_map/reshape | solution.py:51
  489.7 0.0 all-to-all-done.2
  489.7 13.9 %fusion.6 = f32[2,12,1536,64]{2,3,1,0:T(8,128)} fusion(bf16[2,1536,12,128]{3,2,1,0:T(8,128)(2,1)} %reshape.191, bf16[64,2,1536]{2,0,1:T(8,128)(2,1)S(1)} %all-to-all-done.2), kind=kOutput, calls=%fused_computation.13 | convolution fusion | flops 603979776 | bytes 19267584 | tf_op jit(solution)/shard_map/rqhd,rkhd->rhqk/dot_general | solution.py:59
  503.6 0.0 slice-start
  503.6 0.0 slice-start.1
  503.6 0.0 slice-start.2
  503.6 12.1 %fusion.44 = (f32[2,12,64]{2,1,0:T(8,128)S(1)}, bf16[2,12,64,1536]{3,2,1,0:T(8,128)(2,1)}) fusion(f32[2,12,1536,64]{2,3,1,0:T(8,128)} %fusion.6, pred[2,1536]{1,0:T(4,128)(4,1)S(1)} %broadcast_in_dim.42), kind=kOutput, calls=%fused_computation.59 | output fusion | flops 18875904 | bytes 14164992 | tf_op jit(solution)/shard_map/sub | solution.py:64
  515.7 0.0 slice-start.3
  515.7 0.0 slice-start.4
  515.7 11.6 %fusion.24 = bf16[2,64,12,128]{3,1,2,0:T(8,128)(2,1)S(1)} fusion(bf16[2,1536,12,128]{3,2,1,0:T(8,128)(2,1)} %reshape.187, bf16[2,12,64,1536]{3,2,1,0:T(8,128)(2,1)} %get-tuple-element.11, f32[2,64,12]{1,2,0:T(8,128)S(1)} %bitcast.73), kind=kOutput, calls=%fused_computation.23 | convolution fusion | flops 604372992 | bytes 14555136 | tf_op jit(solution)/shard_map/rhqk,rkhd->rqhd/dot_general | solution.py:68
  527.3 0.3 copy.69
  527.6 0.0 copy-start.1
  527.6 0.0 slice-done
  527.6 0.0 slice-done.1
  527.6 0.0 slice-done.2
  527.6 0.0 slice-done.3
  527.6 0.0 slice-done.4
  527.7 3.7 convolution_convert_fusion
  531.4 0.0 reduce-scatter.2.cloned.1.call-update
  531.4 38.8 %reduce-scatter.2.cloned.1.call-done = bf16[64,6144]{1,0:T(8,128)(2,1)} async-done(((bf16[128,6144]{1,0:T(8,128)(2,1)}), bf16[64,6144]{1,0:T(8,128)(2,1)}) %reduce-scatter.2.cloned.1.call-update) | async-done | bytes 786448 | tf_op jit(solution)/shard_map/reduce_scatter | solution.py:73
  570.2 0.0 copy-done.1
  (12 shorter events, 0.1 us)
Async XLA Ops:
  6.5 9.5 %copy-start = (bf16[768,1536]{1,0:T(8,128)(2,1)S(1)}, bf16[768,1536]{1,0:T(8,128)(2,1)}, u32[]{:S(2)}) copy-start(bf16[768,1536]{1,0:T(8,128)(2,1)} %param.8) | copy-start | bytes 7077892
  22.4 6.2 %copy-start.2 = (bf16[768,1536]{1,0:T(8,128)(2,1)S(1)}, bf16[768,1536]{1,0:T(8,128)(2,1)}, u32[]{:S(2)}) copy-start(bf16[768,1536]{1,0:T(8,128)(2,1)} %param.9) | copy-start | bytes 7077892
  22.4 197.2 %all-to-all-start.1 = ((bf16[16,3,64,1536]{3,2,1,0:T(8,128)(2,1)}), bf16[16,3,64,1536]{3,2,1,0:T(8,128)(2,1)}, u32[]{:S(2)}, u32[]{:S(2)}) async-start(bf16[16,3,64,1536]{3,2,1,0:T(8,128)(2,1)} %bitcast.65), calls=%async_computation.1 | async-start | bytes 18874368 | tf_op jit(solution)/shard_map/all_to_all | solution.py:56
  219.7 18.8 %copy-start.3 = (bf16[64,3072]{1,0:T(8,128)(2,1)S(1)}, bf16[64,3072]{1,0:T(8,128)(2,1)}, u32[]{:S(2)}) copy-start(bf16[64,3072]{1,0:T(8,128)(2,1)} %param.7) | copy-start | bytes 1179652
  219.7 209.9 %all-to-all-start = ((bf16[16,3,64,1536]{3,2,1,0:T(8,128)(2,1)}), bf16[16,3,64,1536]{3,2,1,0:T(8,128)(2,1)}, u32[]{:S(2)}, u32[]{:S(2)}) async-start(bf16[16,3,64,1536]{3,2,1,0:T(8,128)(2,1)} %bitcast.64), calls=%async_computation | async-start | bytes 18874368 | tf_op jit(solution)/shard_map/all_to_all | solution.py:57
  429.5 60.2 %all-to-all-start.2 = ((bf16[64,2,1536]{2,0,1:T(8,128)(2,1)}), bf16[64,2,1536]{2,0,1:T(8,128)(2,1)S(1)}, u32[]{:S(2)}, u32[]{:S(2)}) async-start(bf16[64,2,1536]{2,0,1:T(8,128)(2,1)} %bitcast.62), calls=%async_computation.2 | async-start | bytes 786432 | tf_op jit(solution)/shard_map/all_to_all | solution.py:20
  433.5 136.7 %reduce-scatter.2.cloned.1.call-start = ((), (), s32[]{:S(2)}) async-start(), calls=%async_computation.4 | async-start | bytes 2359296 | tf_op jit(solution)/shard_map/reduce_scatter | solution.py:73
  503.6 24.0 %slice-start = ((s8[18874368]{0:T(1024)(128)(4,1)}), s8[2097152]{0:T(1024)(128)(4,1)S(1)}, s32[]{:S(2)}) async-start(s8[18874368]{0:T(1024)(128)(4,1)} %bitcast.67), calls=%async_computation.5 | async-start | bytes 4194304
  503.6 24.0 %slice-start.1 = ((s8[18874368]{0:T(1024)(128)(4,1)}), s8[4194304]{0:T(1024)(128)(4,1)S(1)}, s32[]{:S(2)}) async-start(s8[18874368]{0:T(1024)(128)(4,1)} %bitcast.67), calls=%async_computation.6 | async-start | bytes 8388608
  503.6 24.0 %slice-start.2 = ((s8[18874368]{0:T(1024)(128)(4,1)}), s8[4194304]{0:T(1024)(128)(4,1)S(1)}, s32[]{:S(2)}) async-start(s8[18874368]{0:T(1024)(128)(4,1)} %bitcast.67), calls=%async_computation.7 | async-start | bytes 8388608
  515.7 11.9 %slice-start.3 = ((s8[18874368]{0:T(1024)(128)(4,1)}), s8[4194304]{0:T(1024)(128)(4,1)S(1)}, s32[]{:S(2)}) async-start(s8[18874368]{0:T(1024)(128)(4,1)} %bitcast.67), calls=%async_computation.8 | async-start | bytes 8388608
  515.7 11.9 %slice-start.4 = ((s8[18874368]{0:T(1024)(128)(4,1)}), s8[4194304]{0:T(1024)(128)(4,1)S(1)}, s32[]{:S(2)}) async-start(s8[18874368]{0:T(1024)(128)(4,1)} %bitcast.67), calls=%async_computation.9 | async-start | bytes 8388608
  527.6 42.6 %copy-start.1 = (bf16[768,1536]{1,0:T(8,128)(2,1)S(1)}, bf16[768,1536]{1,0:T(8,128)(2,1)}, u32[]{:S(2)}) copy-start(bf16[768,1536]{1,0:T(8,128)(2,1)} %param.8) | copy-start | bytes 7077892
Sparse Core Ops, SparseCore 0:
  531.5 38.6 reduce-scatter.1
where the time goes:
time: 581 us; the launch traced here: 577 us
  waiting for transfers between devices  414 us (71%)
  local copies, waits for them, and re-layouts  77.6 us (13%)
  matrix products  29.2 us (5%)
  starting transfers between devices  29 us (5%)
  other arithmetic  14.1 us (2%)
  between operations  13.6 us (2%)
    all_to_all x1, waiting for transfers between devices, body(): lax.all_to_all(send_values, 'seq', split_axis=0, concat_axis=0, tiled=True)  190 us
    all_to_all x1, waiting for transfers between devices, body(): lax.all_to_all(send_keys, 'seq', split_axis=0, concat_axis=0, tiled=True)  185 us
    reduce_scatter x1, waiting for transfers between devices, body(): lax.psum_scatter(jnp.dot(attended, w_out, preferred_element_type=jnp.floa...  38.8 us
    reshape x2, local copies, waits for them, and re-layouts, arrange(): return picked_rows.reshape(head_count, MAXSEL * tile_rows, heads_local, HD)  35.6 us
    gather x2, local copies, waits for them, and re-layouts, arrange(): incoming_rows.reshape(seq_count * capacity, tile_rows, width_local)  20.1 us
    all_to_all x1, starting transfers between devices, body(): lax.all_to_all(send_values, 'seq', split_axis=0, concat_axis=0, tiled=True)  18.8 us
    dot_general x1, matrix products, body(): jnp.einsum('rqhd,rkhd->rhqk', query_heads, arrange(recv_keys), preferred_...  13.9 us
    sub x1, other arithmetic, body(): exponent = jnp.where(key_live, jnp.exp(logit_scores - row_top), 0.0)  12.1 us
  transfers between devices with their start and end apart: 4, of which 3 were waited for; matrix products, arithmetic and copies ran while one was open for 11% of the time, Pallas kernels for 0%

commit v1 on v0

v1 whole, which is shorter than its diff:
```python
import functools

import jax
import jax.numpy as jnp
from jax import lax
from jax.experimental import pallas as pl
from jax.experimental.pallas import tpu as pltpu
from jax.sharding import PartitionSpec as P

HD = 128
NEG = -1e30
MESH = pl.DeviceIdType.MESH
VMEM_BUDGET = 58 * 2**20


def grid_of(seq_count):
    rest = seq_count // 2
    y_size = 1
    for y in range(1, rest + 1):
        if rest % y == 0 and y * y <= rest:
            y_size = y
    return rest // y_size, y_size, 2


def split3(x):
    hi = x.astype(jnp.bfloat16)
    rest = x - hi.astype(jnp.float32)
    mid = rest.astype(jnp.bfloat16)
    low = (rest - mid.astype(jnp.float32)).astype(jnp.bfloat16)
    return hi, mid, low


def pack_stats(rows, lanes):
    stacked = jnp.concatenate(rows, axis=0)
    parts = [p.astype(jnp.float32) for p in split3(stacked)]
    pad = jnp.zeros((16 - 3 * len(rows), lanes), jnp.float32)
    return jnp.concatenate(parts + [pad], axis=0).astype(jnp.bfloat16)


def unpack_stats(block, heads):
    wide = block.astype(jnp.float32)
    return wide[:heads] + wide[heads : 2 * heads] + wide[2 * heads : 3 * heads]


def fused_kernel(cfg, *refs):
    (H, Z, Y, C2, hpc, C, cap, T, NQ, F, attn, proj, DN, N) = cfg
    refs = list(refs)
    take = lambda n: [refs.pop(0) for _ in range(n)]
    if attn:
        q_ref, k_ref, v_ref, off_ref, bias_ref = take(5)
    else:
        (att_ref,) = take(1)
    if proj:
        (w_ref,) = take(1)
    (out_ref,) = take(1)
    if attn:
        qbuf, obuf, r_core, r_y, r_z = take(5)
        (local_sem, xs, xr, zs, zr, ys, yr, cs, cr, rcs, rcr, rys, ryr, rzs, rzr) = take(15)
    if proj:
        wbuf, pbuf, r_x = take(3)
        w_sem, ps, pr = take(3)
        if attn:
            (att_ref,) = take(1)

    head = lax.axis_index("head")
    seq = lax.axis_index("seq")
    core = lax.rem(seq, C2)
    y = lax.rem(lax.div(seq, C2), Y)
    z = lax.div(seq, C2 * Y)

    def seq_of(z_at, y_at, core_at):
        return (z_at * Y + y_at) * C2 + core_at

    def peer_head(i):
        return lax.rem(head + i, H)

    def peer_z(i):
        return lax.rem(z + i, Z)

    def peer_y(i):
        return lax.rem(y + i, Y)

    other = 1 - core
    dev_h = lambda i: {"head": peer_head(i)}
    dev_z = lambda i: {"seq": seq_of(peer_z(i), y, core)}
    dev_y = lambda i: {"seq": seq_of(z, peer_y(i), core)}
    dev_c = {"seq": seq_of(z, y, other)}

    if proj:
        def w_copy(n):
            return pltpu.make_async_copy(
                w_ref.at[:, pl.ds(pl.multiple_of(n * DN, DN), DN)], wbuf.at[n], w_sem.at[n]
            )

    barrier = pltpu.get_barrier_semaphore()
    partners = [dev_h(i) for i in range(1, H)]
    if attn:
        partners += [dev_z(i) for i in range(1, Z)] + [dev_y(i) for i in range(1, Y)] + [dev_c]
    for dev in partners:
        pl.semaphore_signal(barrier, inc=1, device_id=dev, device_id_type=MESH)
    pl.semaphore_wait(barrier, len(partners))

    def remote(src, dst, send, recv, dev):
        return pltpu.make_async_remote_copy(
            src_ref=src, dst_ref=dst, send_sem=send, recv_sem=recv, device_id=dev, device_id_type=MESH
        )

    if attn:
        W = C * F
        rows = pl.ds(pl.multiple_of(head * T, T), T)
        mine = lambda c: qbuf.at[c, core, y, z]

        def feature_cols(h_at, c):
            return pl.ds(pl.multiple_of(h_at * W + c * F, F), F)

        def x_local(c):
            return pltpu.make_async_copy(
                q_ref.at[:, feature_cols(head, c)], mine(c).at[rows, :], local_sem.at[c]
            )

        def x_copy(c, i):
            return remote(
                q_ref.at[:, feature_cols(peer_head(i), c)],
                mine(c).at[rows, :],
                xs.at[c, i],
                xr.at[c, i],
                dev_h(i),
            )

        def z_copy(c, i):
            return remote(mine(c), mine(c), zs.at[c, i], zr.at[c, i], dev_z(i))

        def y_copy(c, i):
            return remote(qbuf.at[c, core, y], qbuf.at[c, core, y], ys.at[c, i], yr.at[c, i], dev_y(i))

        def c_copy(c):
            return remote(qbuf.at[c, core], qbuf.at[c, core], cs.at[c], cr.at[c], dev_c)

        def rc_copy(c):
            return remote(obuf.at[c, other], r_core.at[c], rcs.at[c], rcr.at[c], dev_c)

        def ry_copy(c, i):
            return remote(obuf.at[c, core, peer_y(i)], r_y.at[c, i - 1], rys.at[c, i], ryr.at[c, i], dev_y(i))

        def rz_copy(c, i):
            return remote(obuf.at[c, core, y, peer_z(i)], r_z.at[c, i - 1], rzs.at[c, i], rzr.at[c, i], dev_z(i))

        def merged(blocks, h):
            stats = [s[h : h + 1] for _, s in blocks]
            top = functools.reduce(jnp.maximum, stats)
            weight = [jnp.exp(s - top) for s in stats]
            total = functools.reduce(jnp.add, weight)
            inverse = 1.0 / total
            o = None
            for (block, _), w in zip(blocks, weight):
                part = block[h * HD : (h + 1) * HD, :].astype(jnp.float32) * (w * inverse)
                o = part if o is None else o + part
            return o, top + jnp.log(total)

        def merge_into(dst, sources):
            blocks = [(r, unpack_stats(r[F : F + 16, :], hpc)) for r in [dst] + sources]
            logs = []
            for h in range(hpc):
                o, log = merged(blocks, h)
                dst[h * HD : (h + 1) * HD, :] = o.astype(jnp.bfloat16)
                logs.append(log)
            dst[F : F + 16, :] = pack_stats(logs, NQ)

        scale = HD ** -0.5

        def compute(c):
            @pl.loop(0, C2 * Y * Z)
            def _(g):
                g_core = lax.div(g, Y * Z)
                g_y = lax.rem(lax.div(g, Z), Y)
                g_z = lax.rem(g, Z)
                group = (g_z * Y + g_y) * C2 + g_core
                starts = [off_ref[group * cap + r] for r in range(cap)]
                bias = bias_ref[group]
                logs = []
                for h in range(hpc):
                    cols = slice(c * F + h * HD, c * F + (h + 1) * HD)
                    qh = qbuf[c, g_core, g_y, g_z, :, h * HD : (h + 1) * HD]
                    keys = jnp.concatenate([k_ref[s, :, cols] for s in starts], axis=0)
                    vals = jnp.concatenate([v_ref[s, :, cols] for s in starts], axis=0)
                    scores = lax.dot_general(
                        keys, qh, (((1,), (1,)), ((), ())), preferred_element_type=jnp.float32
                    )
                    scores = jnp.concatenate(
                        [scores[r * T : (r + 1) * T] * scale + bias[r : r + 1] for r in range(cap)], axis=0
                    )
                    top = jnp.max(scores, axis=0, keepdims=True)
                    exponent = jnp.exp(scores - top)
                    total = jnp.sum(exponent, axis=0, keepdims=True)
                    o = lax.dot_general(
                        vals,
                        exponent.astype(jnp.bfloat16),
                        (((0,), (0,)), ((), ())),
                        preferred_element_type=jnp.float32,
                    )
                    obuf[c, g_core, g_y, g_z, h * HD : (h + 1) * HD, :] = (o * (1.0 / total)).astype(jnp.bfloat16)
                    logs.append(top + jnp.log(total))
                obuf[c, g_core, g_y, g_z, F : F + 16, :] = pack_stats(logs, NQ)

        def start_x(c):
            x_local(c).start()
            for i in range(1, H):
                x_copy(c, i).start()

        def step_x(c):
            x_local(c).wait()
            for i in range(1, H):
                rows_in = pl.ds(pl.multiple_of(lax.rem(head - i + H, H) * T, T), T)
                remote(mine(c).at[rows_in, :], mine(c).at[rows_in, :], xs.at[c, i], xr.at[c, i], dev_h(i)).wait_recv()
            for i in range(1, Z):
                z_copy(c, i).start()

        def step_z(c):
            for i in range(1, Z):
                slot = qbuf.at[c, core, y, lax.rem(z - i + Z, Z)]
                remote(slot, slot, zs.at[c, i], zr.at[c, i], dev_z(i)).wait_recv()
            for i in range(1, Y):
                y_copy(c, i).start()

        def step_y(c):
            for i in range(1, Y):
                slot = qbuf.at[c, core, lax.rem(y - i + Y, Y)]
                remote(slot, slot, ys.at[c, i], yr.at[c, i], dev_y(i)).wait_recv()
            c_copy(c).start()

        def step_compute(c):
            slot = qbuf.at[c, other]
            remote(slot, slot, cs.at[c], cr.at[c], dev_c).wait_recv()
            compute(c)
            rc_copy(c).start()

        def step_rc(c):
            rc_copy(c).wait_recv()

            @pl.loop(0, Y * Z)
            def _(g):
                g_y, g_z = lax.div(g, Z), lax.rem(g, Z)
                merge_into(obuf.at[c, core, g_y, g_z], [r_core.at[c, g_y, g_z]])

            for i in range(1, Y):
                ry_copy(c, i).start()

        def step_ry(c):
            for i in range(1, Y):
                ry_copy(c, i).wait_recv()

            @pl.loop(0, Z)
            def _(g_z):
                merge_into(obuf.at[c, core, y, g_z], [r_y.at[c, i, g_z] for i in range(Y - 1)])

            for i in range(1, Z):
                rz_copy(c, i).start()

        att_out = att_ref if proj else out_ref

        def step_rz(c):
            for i in range(1, Z):
                rz_copy(c, i).wait_recv()
            sources = [obuf.at[c, core, y, z]] + [r_z.at[c, i] for i in range(Z - 1)]
            blocks = [(r, unpack_stats(r[F : F + 16, :], hpc)) for r in sources]
            for h in range(hpc):
                o, _ = merged(blocks, h)
                cols = slice(c * F + h * HD, c * F + (h + 1) * HD)
                att_out[:, cols] = jnp.transpose(o).astype(jnp.bfloat16)

        for c in range(C):
            start_x(c)
        if proj:
            @pl.loop(0, N)
            def _(n):
                w_copy(n).start()
        steps = (step_x, step_z, step_y, step_compute, step_rc, step_ry, step_rz)
        for t in range(C + len(steps) - 1):
            for at, step in enumerate(steps):
                if 0 <= t - at < C:
                    step(t - at)
        for c in range(C):
            for i in range(1, H):
                x_copy(c, i).wait_send()
            for i in range(1, Z):
                z_copy(c, i).wait_send()
                rz_copy(c, i).wait_send()
            for i in range(1, Y):
                y_copy(c, i).wait_send()
                ry_copy(c, i).wait_send()
            c_copy(c).wait_send()
            rc_copy(c).wait_send()
    else:
        @pl.loop(0, N)
        def _(n):
            w_copy(n).start()

    if proj:
        def p_copy(n, i):
            return remote(pbuf.at[n, peer_head(i)], r_x.at[n, i - 1], ps.at[n, i], pr.at[n, i], dev_h(i))

        @pl.loop(0, N)
        def _(n):
            w_copy(n).wait()
            part = jnp.dot(att_ref[...], wbuf[n], preferred_element_type=jnp.float32).astype(jnp.bfloat16)
            for h in range(H):
                pbuf[n, h] = part[h * T : (h + 1) * T]
            for i in range(1, H):
                p_copy(n, i).start()

        @pl.loop(0, N)
        def _(n):
            for i in range(1, H):
                p_copy(n, i).wait_recv()
            total = pbuf[n, head].astype(jnp.float32)
            for i in range(H - 1):
                total = total + r_x[n, i].astype(jnp.float32)
            out_ref[:, pl.ds(pl.multiple_of(n * DN, DN), DN)] = total.astype(jnp.bfloat16)
            for i in range(1, H):
                p_copy(n, i).wait_send()


def run_kernel(H, S, T, W, D, cap, kv_rows, attn, proj, operands, cid):
    Z, Y, C2 = grid_of(S)
    NQ = H * T
    heads = W // HD
    hpc = next(n for n in (3, 2, 1) if heads % n == 0)
    C = heads // hpc
    F = hpc * HD
    DN = 512
    N = D // DN
    cfg = (H, Z, Y, C2, hpc, C, cap, T, NQ, F, attn, proj, DN, N)
    bf, dma = jnp.bfloat16, pltpu.SemaphoreType.DMA
    vmem, hbm = pl.BlockSpec(memory_space=pltpu.VMEM), pl.BlockSpec(memory_space=pl.ANY)
    in_specs, scratch = [], []
    if attn:
        in_specs += [vmem, vmem, vmem, pl.BlockSpec(memory_space=pltpu.SMEM), vmem]
        scratch += [
            pltpu.VMEM((C, C2, Y, Z, NQ, F), bf),
            pltpu.VMEM((C, C2, Y, Z, F + 16, NQ), bf),
            pltpu.VMEM((C, Y, Z, F + 16, NQ), bf),
            pltpu.VMEM((C, Y - 1, Z, F + 16, NQ), bf),
            pltpu.VMEM((C, Z - 1, F + 16, NQ), bf),
        ]
        scratch += [dma((C,)), dma((C, H)), dma((C, H)), dma((C, Z)), dma((C, Z)), dma((C, Y)), dma((C, Y))]
        scratch += [dma((C,))] * 4 + [dma((C, Y)), dma((C, Y)), dma((C, Z)), dma((C, Z))]
    else:
        in_specs += [vmem]
    if proj:
        in_specs += [hbm]
        scratch += [
            pltpu.VMEM((N, W, DN), bf),
            pltpu.VMEM((N, H, T, DN), bf),
            pltpu.VMEM((N, H - 1, T, DN), bf),
            dma((N,)),
            dma((N, H)),
            dma((N, H)),
        ]
        if attn:
            scratch += [pltpu.VMEM((NQ, W), bf)]
        out = jax.ShapeDtypeStruct((T, D), bf)
    else:
        out = jax.ShapeDtypeStruct((NQ, W), bf)
    flops = 0
    if attn:
        flops += 4 * S * NQ * cap * T * W
    if proj:
        flops += 2 * NQ * W * D
    return pl.pallas_call(
        functools.partial(fused_kernel, cfg),
        out_shape=out,
        in_specs=in_specs,
        out_specs=vmem,
        scratch_shapes=scratch,
        cost_estimate=pl.CostEstimate(flops=flops, bytes_accessed=2 * (2 * kv_rows * W + W * D), transcendentals=0),
        compiler_params=pltpu.CompilerParams(
            collective_id=cid, has_side_effects=True, vmem_limit_bytes=VMEM_BUDGET
        ),
    )(*operands)


def body(queries, key_rows, values, w_out, picked, counts, tile_home):
    H, S = lax.axis_size("head"), lax.axis_size("seq")
    seq = lax.axis_index("seq")
    T = queries.shape[0]
    W, D = w_out.shape
    kv_rows = key_rows.shape[0]
    tiles_dev = kv_rows // T
    most = picked.shape[1]
    cap = max(2, H * most // S)
    entries = H * most
    tiles = lax.broadcasted_iota(jnp.int32, (1, 1, tile_home.shape[0]), 2)
    stored = jnp.sum(jnp.where(picked[:, :, None] == tiles, tile_home[None, None, :], 0), axis=2)
    live = lax.broadcasted_iota(jnp.int32, picked.shape, 1) < counts[:, None]
    hit = (live & (stored // tiles_dev == seq)).astype(jnp.int32)
    hit = hit.reshape(H, S, most).transpose(1, 0, 2).reshape(S, entries)
    inside = (stored % tiles_dev).reshape(H, S, most).transpose(1, 0, 2).reshape(S, entries)
    at = lax.broadcasted_iota(jnp.int32, (1, entries, entries), 1)
    before = lax.broadcasted_iota(jnp.int32, (1, entries, entries), 2)
    rank = jnp.sum(jnp.where(before < at, hit[:, None, :], 0), axis=2)
    slot = lax.broadcasted_iota(jnp.int32, (1, cap, 1), 1)
    chosen = (hit[:, None, :] > 0) & (rank[:, None, :] == slot)
    offsets = jnp.sum(jnp.where(chosen, inside[:, None, :], 0), axis=2).reshape(S * cap)
    wanted_by = chosen.reshape(S, cap, H, most).any(axis=3)
    bias = jnp.where(jnp.repeat(wanted_by, T, axis=2), 0.0, NEG).astype(jnp.float32)
    bias = jnp.pad(bias, ((0, 0), (0, 8 - cap), (0, 0)))

    key_tiles = key_rows.reshape(tiles_dev, T, W)
    value_tiles = values.reshape(tiles_dev, T, W)
    call = functools.partial(run_kernel, H, S, T)
    whole_bytes = 2 * (2 * S * H * T * W * 2 + 2 * kv_rows * W + W * D)
    if whole_bytes < 52 * 2**20:
        return call(W, D, cap, kv_rows, True, True, (queries, key_tiles, value_tiles, offsets, bias, w_out), 1)
    heads = W // HD
    per = max(n for n in range(1, heads + 1) if heads % n == 0 and 7 * S * H * T * n * HD < 30 * 2**20)
    width = per * HD
    columns = queries.reshape(T, H, W)
    pieces = []
    for p in range(heads // per):
        at = slice(p * width, (p + 1) * width)
        pieces.append(
            call(
                width, D, cap, kv_rows, True, False,
                (columns[:, :, at].reshape(T, H * width), key_tiles[:, :, at], value_tiles[:, :, at], offsets, bias), 1,
            )
        )
    return call(W, D, cap, kv_rows, False, True, (jnp.concatenate(pieces, axis=1), w_out), 2)


def solution(mesh):
    placed = (
        P(("head", "seq"), None),
        P("seq", "head"),
        P("seq", "head"),
        P("head", None),
        P(),
        P(),
        P(),
    )
    return jax.shard_map(
        body, mesh=mesh, in_specs=placed, out_specs=P(("head", "seq"), None), check_vma=False
    )
```

time: 581 us -> 150 us (0.26)
  waiting for transfers between devices: 414 us -> 0 us
  Pallas kernels: 0 us -> 142 us
  local copies, waits for them, and re-layouts: 77.6 us -> 5.56 us
  matrix products: 29.2 us -> 0 us
  starting transfers between devices: 29 us -> 0 us
  between operations: 13.6 us -> 0.09 us
  other arithmetic: 14.1 us -> 2.23 us
    all_to_all x3 -> x0, waiting for transfers between devices: 375 us -> none  [the longest x1 190 us: body(): lax.all_to_all(send_values, 'seq', split_axis=0, concat_axis=0, tiled=True)]
    pallas_call x0 -> x1, Pallas kernels: none -> 142 us  [run_kernel(): pl.pallas_call(functools.partial(fused_kernel, cfg), out_shape=out, in_sp...]
    reduce_scatter x1 -> x0, waiting for transfers between devices: 38.8 us -> none  [body(): lax.psum_scatter(jnp.dot(attended, w_out, preferred_element_type=jnp.floa...]
    gather x5 -> x0, local copies, waits for them, and re-layouts: 37.7 us -> none  [the longest x2 20.1 us: arrange(): incoming_rows.reshape(seq_count * capacity, tile_rows, width_local)]
    reshape x5 -> x1, local copies, waits for them, and re-layouts: 36.5 us -> 0.68 us  [body(): jnp.sum(jnp.where(chosen, inside[:, None, :], 0), axis=2).reshape(S * cap)]
    dot_general x3 -> x0, matrix products: 29.2 us -> none  [the longest x1 13.9 us: body(): jnp.einsum('rqhd,rkhd->rhqk', query_heads, arrange(recv_keys), preferred_...]
    all_to_all x3 -> x0, starting transfers between devices: 29 us -> none  [the longest x1 18.8 us: body(): lax.all_to_all(send_values, 'seq', split_axis=0, concat_axis=0, tiled=True)]
    sub x1 -> x0, other arithmetic: 12.1 us -> none  [body(): exponent = jnp.where(key_live, jnp.exp(logit_scores - row_top), 0.0)]
  transfers between devices with their start and end apart: 4 -> 0, of which waited for: 3 -> 0; matrix products, arithmetic and copies ran while one was open for 11% -> 0% of each run, Pallas kernels for 0% -> 0%
where the time goes in v1:
time: 150 us
  Pallas kernels  142 us (95%)
  local copies, waits for them, and re-layouts  5.56 us (4%)
  other arithmetic  2.23 us (1%)
    pallas_call x1, Pallas kernels, run_kernel(): pl.pallas_call(functools.partial(fused_kernel, cfg), out_shape=out, in_sp...  142 us

profile of v1, /device:TPU:26, one launch (start us, length us, event | category | flops | bytes accessed | tf_op | source)
XLA Modules:
  0.0 149.8 jit_solution(11255282925032719983)
XLA Ops:
  0.0 0.7 lt.25
  0.7 0.8 copy.18
  1.5 1.4 select_reduce_fusion
  3.0 0.1 broadcast_compare_fusion
  3.1 0.1 broadcast_in_dim.66
  3.2 0.1 broadcast_in_dim_reshape.2
  3.3 0.3 select_reduce_fusion.1
  3.6 0.1 select_reduce_fusion.2
  3.8 0.1 copy.21
  3.9 0.7 reshape.57.refs_3_
  4.5 0.1 eq.52
  4.6 0.2 fusion.1
  4.8 0.1 copy.23
  4.9 0.1 broadcast_in_dim.71
  5.1 0.1 select_n.40
  5.2 0.6 pad.4.refs_4_
  5.8 141.9 %shard_map.73 = bf16[64,6144]{1,0:T(8,128)(2,1)} custom-call(bf16[64,3072]{1,0:T(8,128)(2,1)} %refs_0_.1, bf16[12,64,1536]{2,1,0:T(8,128)(2,1)} %bitcast.12, bf16[12,64,1536]{2,1,0:T(8,128)(2,1)} %bitcast.13, s32[48]{0:T(128)} %reshape.57.refs_3_, f32[16,8,128]{2,1,0:T(8,128)} %pad.4.refs_4_, bf16[1536,6144]{1,0:T(8,128)(2,1)} %refs_5_.1), custom_call_target="tpu_custom_call" | custom-call | flops 4831838208 | bytes 23592960 | tf_op jit(solution)/shard_map/pallas_call | solution.py:369
  147.7 2.1 %copy.26 = bf16[64,6144]{1,0:T(8,128)(2,1)} copy(bf16[64,6144]{1,0:T(8,128)(2,1)} %shard_map.73) | data formatting | bytes 1572864
  (10 shorter events, 0.1 us)

commit v2 on v1

--- a/solution.py
+++ b/solution.py
@@ -169,7 +169,7 @@
         scale = HD ** -0.5
 
         def compute(c):
-            @pl.loop(0, C2 * Y * Z)
+            @pl.loop(0, C2 * Y * Z, unroll=2)
             def _(g):
                 g_core = lax.div(g, Y * Z)
                 g_y = lax.rem(lax.div(g, Z), Y)
@@ -177,29 +177,37 @@
                 group = (g_z * Y + g_y) * C2 + g_core
                 starts = [off_ref[group * cap + r] for r in range(cap)]
                 bias = bias_ref[group]
-                logs = []
+                cols = [slice(c * F + h * HD, c * F + (h + 1) * HD) for h in range(hpc)]
+                raw = []
                 for h in range(hpc):
-                    cols = slice(c * F + h * HD, c * F + (h + 1) * HD)
                     qh = qbuf[c, g_core, g_y, g_z, :, h * HD : (h + 1) * HD]
-                    keys = jnp.concatenate([k_ref[s, :, cols] for s in starts], axis=0)
-                    vals = jnp.concatenate([v_ref[s, :, cols] for s in starts], axis=0)
-                    scores = lax.dot_general(
-                        keys, qh, (((1,), (1,)), ((), ())), preferred_element_type=jnp.float32
+                    keys = jnp.concatenate([k_ref[s, :, cols[h]] for s in starts], axis=0)
+                    raw.append(
+                        lax.dot_general(keys, qh, (((1,), (1,)), ((), ())), preferred_element_type=jnp.float32)
                     )
+                weights, totals, logs = [], [], []
+                for h in range(hpc):
                     scores = jnp.concatenate(
-                        [scores[r * T : (r + 1) * T] * scale + bias[r : r + 1] for r in range(cap)], axis=0
+                        [raw[h][r * T : (r + 1) * T] * scale + bias[r : r + 1] for r in range(cap)], axis=0
                     )
                     top = jnp.max(scores, axis=0, keepdims=True)
                     exponent = jnp.exp(scores - top)
                     total = jnp.sum(exponent, axis=0, keepdims=True)
-                    o = lax.dot_general(
-                        vals,
-                        exponent.astype(jnp.bfloat16),
-                        (((0,), (0,)), ((), ())),
-                        preferred_element_type=jnp.float32,
+                    weights.append(exponent.astype(jnp.bfloat16))
+                    totals.append(total)
+                    logs.append(top + jnp.log(total))
+                mixed = []
+                for h in range(hpc):
+                    vals = jnp.concatenate([v_ref[s, :, cols[h]] for s in starts], axis=0)
+                    mixed.append(
+                        lax.dot_general(
+                            vals, weights[h], (((0,), (0,)), ((), ())), preferred_element_type=jnp.float32
+                        )
                     )
-                    obuf[c, g_core, g_y, g_z, h * HD : (h + 1) * HD, :] = (o * (1.0 / total)).astype(jnp.bfloat16)
-                    logs.append(top + jnp.log(total))
+                for h in range(hpc):
+                    obuf[c, g_core, g_y, g_z, h * HD : (h + 1) * HD, :] = (
+                        mixed[h] * (1.0 / totals[h])
+                    ).astype(jnp.bfloat16)
                 obuf[c, g_core, g_y, g_z, F : F + 16, :] = pack_stats(logs, NQ)
 
         def start_x(c):
@@ -324,7 +332,7 @@
     Z, Y, C2 = grid_of(S)
     NQ = H * T
     heads = W // HD
-    hpc = next(n for n in (3, 2, 1) if heads % n == 0)
+    hpc = next(n for n in (2, 1) if heads % n == 0)
     C = heads // hpc
     F = hpc * HD
     DN = 512

time: 150 us -> 129 us (0.86)
  Pallas kernels: 142 us -> 121 us
    pallas_call x1, Pallas kernels: 142 us -> 121 us  [run_kernel(): pl.pallas_call(functools.partial(fused_kernel, cfg), out_shape=out, in_sp...]
where the time goes in v2:
time: 129 us
  Pallas kernels  121 us (94%)
  local copies, waits for them, and re-layouts  5.56 us (4%)
  other arithmetic  2.23 us (2%)
    pallas_call x1, Pallas kernels, run_kernel(): pl.pallas_call(functools.partial(fused_kernel, cfg), out_shape=out, in_sp...  121 us
    unnamed x2, local copies, waits for them, and re-layouts  2.84 us

profile of v2, /device:TPU:26, one launch (start us, length us, event | category | flops | bytes accessed | tf_op | source)
XLA Modules:
  0.0 129.1 jit_solution(6896112976808480503)
XLA Ops:
  0.0 0.7 lt.25
  0.7 0.8 copy.18
  1.5 1.4 %select_reduce_fusion = s32[32,24]{1,0:T(8,128)S(1)} fusion(s32[192]{0:T(256)} %param.13, s32[32,24]{1,0:T(8,128)S(1)} %copy.18), kind=kLoop, calls=%fused_computation | loop fusion | flops 441600 | bytes 6912 | tf_op jit(solution)/shard_map/reduce_sum | solution.py:401
  3.0 0.1 broadcast_compare_fusion
  3.1 0.1 broadcast_in_dim.66
  3.2 0.1 broadcast_in_dim_reshape.2
  3.3 0.3 select_reduce_fusion.1
  3.6 0.1 select_reduce_fusion.2
  3.8 0.1 copy.21
  3.9 0.7 reshape.57.refs_3_
  4.5 0.1 eq.52
  4.6 0.2 fusion.1
  4.8 0.1 copy.23
  4.9 0.1 broadcast_in_dim.71
  5.1 0.1 select_n.40
  5.2 0.6 pad.4.refs_4_
  5.8 121.2 %shard_map.73 = bf16[64,6144]{1,0:T(8,128)(2,1)} custom-call(bf16[64,3072]{1,0:T(8,128)(2,1)} %refs_0_.1, bf16[12,64,1536]{2,1,0:T(8,128)(2,1)} %bitcast.12, bf16[12,64,1536]{2,1,0:T(8,128)(2,1)} %bitcast.13, s32[48]{0:T(128)} %reshape.57.refs_3_, f32[16,8,128]{2,1,0:T(8,128)} %pad.4.refs_4_, bf16[1536,6144]{1,0:T(8,128)(2,1)} %refs_5_.1), custom_call_target="tpu_custom_call" | custom-call | flops 4831838208 | bytes 23592960 | tf_op jit(solution)/shard_map/pallas_call | solution.py:377
  127.1 2.1 %copy.26 = bf16[64,6144]{1,0:T(8,128)(2,1)} copy(bf16[64,6144]{1,0:T(8,128)(2,1)} %shard_map.73) | data formatting | bytes 1572864
  (10 shorter events, 0.1 us)

commit v3 on v2

--- a/solution.py
+++ b/solution.py
@@ -169,7 +169,7 @@
         scale = HD ** -0.5
 
         def compute(c):
-            @pl.loop(0, C2 * Y * Z, unroll=2)
+            @pl.loop(0, C2 * Y * Z, unroll=4)
             def _(g):
                 g_core = lax.div(g, Y * Z)
                 g_y = lax.rem(lax.div(g, Z), Y)

time: 129 us -> 128 us (level)
    pallas_call x1, Pallas kernels: 121 us -> 120 us  [run_kernel(): pl.pallas_call(functools.partial(fused_kernel, cfg), out_shape=out, in_sp...]
where the time goes in v3:
time: 128 us
  Pallas kernels  120 us (94%)
  local copies, waits for them, and re-layouts  5.56 us (4%)
  other arithmetic  2.23 us (2%)
    pallas_call x1, Pallas kernels, run_kernel(): pl.pallas_call(functools.partial(fused_kernel, cfg), out_shape=out, in_sp...  120 us
    unnamed x2, local copies, waits for them, and re-layouts  2.84 us

profile of v3, /device:TPU:26, one launch (start us, length us, event | category | flops | bytes accessed | tf_op | source)
XLA Modules:
  0.0 127.7 jit_solution(7807487758387822332)
XLA Ops:
  0.0 0.7 lt.25
  0.7 0.8 copy.18
  1.5 1.4 %select_reduce_fusion = s32[32,24]{1,0:T(8,128)S(1)} fusion(s32[192]{0:T(256)} %param.13, s32[32,24]{1,0:T(8,128)S(1)} %copy.18), kind=kLoop, calls=%fused_computation | loop fusion | flops 441600 | bytes 6912 | tf_op jit(solution)/shard_map/reduce_sum | solution.py:401
  3.0 0.1 broadcast_compare_fusion
  3.1 0.1 broadcast_in_dim.66
  3.2 0.1 broadcast_in_dim_reshape.2
  3.3 0.3 select_reduce_fusion.1
  3.6 0.1 select_reduce_fusion.2
  3.8 0.1 copy.21
  3.9 0.7 reshape.57.refs_3_
  4.5 0.1 eq.52
  4.6 0.2 fusion.1
  4.8 0.1 copy.23
  4.9 0.1 broadcast_in_dim.71
  5.1 0.1 select_n.40
  5.2 0.6 pad.4.refs_4_
  5.8 119.8 %shard_map.73 = bf16[64,6144]{1,0:T(8,128)(2,1)} custom-call(bf16[64,3072]{1,0:T(8,128)(2,1)} %refs_0_.1, bf16[12,64,1536]{2,1,0:T(8,128)(2,1)} %bitcast.12, bf16[12,64,1536]{2,1,0:T(8,128)(2,1)} %bitcast.13, s32[48]{0:T(128)} %reshape.57.refs_3_, f32[16,8,128]{2,1,0:T(8,128)} %pad.4.refs_4_, bf16[1536,6144]{1,0:T(8,128)(2,1)} %refs_5_.1), custom_call_target="tpu_custom_call" | custom-call | flops 4831838208 | bytes 23592960 | tf_op jit(solution)/shard_map/pallas_call | solution.py:377
  125.6 2.1 %copy.26 = bf16[64,6144]{1,0:T(8,128)(2,1)} copy(bf16[64,6144]{1,0:T(8,128)(2,1)} %shard_map.73) | data formatting | bytes 1572864
  (10 shorter events, 0.1 us)
